TPU v7x, 256 devices: a whole 4x4x8 slice. The times are simulated.
256 devices in a mesh: sect: 2 (over x_hi), dev: 64 (over y, x_lo, z), cores: 2 (over core).
Axes of the slice: x: 4 (x_hi: 2, x_lo: 2; x = x_hi * 2 + x_lo), y: 4, z: 8, core: 2. Of those that a mesh axis runs over, the one named last changes fastest.
Arguments:
- query: bfloat16 [3072, 8192], P(('sect', 'dev'), 'cores'), may hold values from -30 to 30
- cache_keys: bfloat16 [3072, 128, 512], P(('sect', 'dev'), None, 'cores'), may hold values from -6 to 6
- cache_values: bfloat16 [3072, 128, 512], P(('sect', 'dev'), None, 'cores'), may hold values from -6 to 6
- new_key: bfloat16 [3072, 512], P(('sect', 'dev'), 'cores'), may hold values from -6 to 6
- new_value: bfloat16 [3072, 512], P(('sect', 'dev'), 'cores'), may hold values from -6 to 6
- lengths: int32 [3072], P(('sect', 'dev')), may hold values from 1 to 128
- hidden: bfloat16 [3072, 4096], P(('sect', 'dev')), may hold values from -6 to 6
- routes: int32 [3072, 8], P(('sect', 'dev')), may hold values from 0 to 63, all different within a row; in each aligned block of 24 rows (0 to 23, 24 to 47, ...) at most 6 rows name the same one
- gate_weights: float32 [3072, 8], P(('sect', 'dev')), may hold values from 0.1 to 1
- w_gate: bfloat16 [64, 4096, 1536], P('dev', None, ('sect', 'cores')), may hold values from -0.09375 to 0.09375
- w_up: bfloat16 [64, 4096, 1536], P('dev', None, ('sect', 'cores')), may hold values from -0.09375 to 0.09375
- w_down: bfloat16 [64, 4096, 1536], P('dev', None, ('sect', 'cores')), may hold values from -0.15625 to 0.15625
Outputs:
- attended: bfloat16 [3072, 8192], P(('sect', 'dev'), 'cores')
- expert_out: bfloat16 [3072, 4096], P(('sect', 'dev'), 'cores')
Inputs may be any that keep to these rules, and one draw needn't show every extreme that they name: Each row names 8 different experts; the rows of one aligned block of 24 send at most 6 routes to one expert.
All inputs are finite; a program needn't handle non-finite values.
Results may differ from a plain program's by a relative error of at most 0.0075.
Values may be sent and summed in bfloat16 or wider, within the bound.
A program may use at most 128 MiB of HBM per device.

v0:
```python
import jax
import jax.numpy as jnp
from jax import lax
from jax.sharding import PartitionSpec as P

HD = 128


def block_slots(routes, experts, capacity):
    rows, topk = routes.shape
    flat = routes.reshape(rows * topk)
    onehot = (flat[:, None] == jnp.arange(experts, dtype=jnp.int32)[None, :]).astype(jnp.int32)
    before = jnp.cumsum(onehot, axis=0) - onehot
    slot = jnp.sum(before * onehot, axis=1)
    return (flat * capacity + slot).reshape(rows, topk)


def attend(query, cache_keys, cache_values, new_key, new_value, lengths):
    rows = query.shape[0]
    length = cache_keys.shape[1]
    heads_here = query.shape[1] // HD
    kv_here = new_key.shape[1] // HD
    group = heads_here // kv_here
    scale = HD ** (-0.5)
    q_heads = query.reshape(rows, kv_here, group, HD)
    keys = cache_keys.reshape(rows, length, kv_here, HD)
    values = cache_values.reshape(rows, length, kv_here, HD)
    scores = (
        jnp.einsum("rkgd,rlkd->rkgl", q_heads, keys, preferred_element_type=jnp.float32) * scale
    )
    valid = jnp.arange(length, dtype=jnp.int32)[None, :] < lengths[:, None]
    scores = jnp.where(valid[:, None, None, :], scores, -jnp.inf)
    own = (
        jnp.einsum(
            "rkgd,rkd->rkg",
            q_heads,
            new_key.reshape(rows, kv_here, HD),
            preferred_element_type=jnp.float32,
        )
        * scale
    )
    top = jnp.maximum(jnp.max(scores, axis=-1), own)
    probs = jnp.exp(scores - top[..., None])
    own_p = jnp.exp(own - top)
    total = jnp.sum(probs, axis=-1) + own_p
    probs_b = (probs / total[..., None]).astype(jnp.bfloat16)
    own_b = (own_p / total).astype(jnp.bfloat16)
    mixed = jnp.einsum("rkgl,rlkd->rkgd", probs_b, values, preferred_element_type=jnp.float32)
    mixed = mixed + own_b.astype(jnp.float32)[..., None] * new_value.astype(jnp.float32).reshape(
        rows, kv_here, 1, HD
    )
    return mixed.astype(jnp.bfloat16).reshape(rows, heads_here * HD)


def per_device(
    query,
    cache_keys,
    cache_values,
    new_key,
    new_value,
    lengths,
    hidden,
    routes,
    gate_weights,
    w_gate,
    w_up,
    w_down,
):
    experts = lax.axis_size("dev")
    sections = lax.axis_size("sect")
    cores = lax.axis_size("cores")
    rows = hidden.shape[0]
    width = hidden.shape[1]
    topk = routes.shape[1]
    half = width // cores
    capacity = min(rows, max(2, 2 * rows * topk // experts))
    slots_all = experts * capacity
    places = block_slots(routes, experts, capacity)
    chosen = places.reshape(-1)[None, :] == jnp.arange(slots_all, dtype=jnp.int32)[:, None]
    pick = jnp.any(chosen.reshape(slots_all, rows, topk), axis=2).astype(jnp.bfloat16)
    outgoing = jnp.dot(pick, hidden, preferred_element_type=jnp.float32).astype(jnp.bfloat16)
    arrived = lax.all_to_all(
        outgoing.reshape(experts, capacity, width), "dev", split_axis=0, concat_axis=0, tiled=True
    )
    local_rows = arrived.reshape(slots_all, width)
    attended = attend(query, cache_keys, cache_values, new_key, new_value, lengths)
    gate_w = w_gate[0]
    up_w = w_up[0]
    down_w = w_down[0]
    inner_width = gate_w.shape[1]
    piece = lax.all_gather(local_rows, "sect", axis=0, tiled=True)
    gate = jnp.dot(piece, gate_w, preferred_element_type=jnp.float32)
    up = jnp.dot(piece, up_w, preferred_element_type=jnp.float32)
    inner = (jax.nn.silu(gate) * up).astype(jnp.bfloat16)
    terms = jnp.einsum(
        "snf,cdf->scnd",
        inner.reshape(sections, slots_all, inner_width),
        down_w.reshape(cores, half, inner_width),
        preferred_element_type=jnp.float32,
    )
    summed = lax.psum_scatter(
        terms.reshape(sections * cores * slots_all, half),
        ("sect", "cores"),
        scatter_dimension=0,
        tiled=True,
    )
    result = summed.astype(jnp.bfloat16).reshape(experts, capacity, half)
    returned = lax.all_to_all(result, "dev", split_axis=0, concat_axis=0, tiled=True)
    flat = returned.reshape(slots_all, half)
    picked = flat[places].astype(jnp.float32)
    expert_out = jnp.sum(picked * gate_weights[:, :, None], axis=1).astype(jnp.bfloat16)
    return (attended, expert_out)


def solution(mesh):
    in_specs = (
        P(("sect", "dev"), "cores"),
        P(("sect", "dev"), None, "cores"),
        P(("sect", "dev"), None, "cores"),
        P(("sect", "dev"), "cores"),
        P(("sect", "dev"), "cores"),
        P(("sect", "dev")),
        P(("sect", "dev"), None),
        P(("sect", "dev"), None),
        P(("sect", "dev"), None),
        P("dev", None, ("sect", "cores")),
        P("dev", None, ("sect", "cores")),
        P("dev", None, ("sect", "cores")),
    )
    out_specs = (P(("sect", "dev"), "cores"), P(("sect", "dev"), "cores"))
    return jax.shard_map(
        per_device, mesh=mesh, in_specs=in_specs, out_specs=out_specs, check_vma=False
    )
```

profile of v0, /device:TPU:2, one launch (start us, length us, event | category | flops | bytes accessed | tf_op | source)
XLA Modules:
  0.0 430.0 jit_solution(4839990486176436913)
XLA Ops:
  7.2 0.9 copy.27
  8.1 0.1 eq.36
  8.3 0.6 reduce-window.6
  8.9 0.2 slice_reduce_fusion
  9.1 0.1 bitcast_bitcast_fusion
  9.2 0.1 reduce_sum.31
  9.3 0.2 fusion.30
  9.5 3.6 convolution_convert_fusion
  13.1 5.6 %reshape.99 = bf16[64,6,4096]{2,1,0:T(8,128)(2,1)} reshape(bf16[384,4096]{1,0:T(8,128)(2,1)} %convolution_convert_fusion) | data formatting | bytes 6291456 | tf_op jit(solution)/shard_map/reshape | solution.py:83
  18.8 108.3 %all_to_all.10 = bf16[64,6,4096]{2,1,0:T(8,128)(2,1)} all-to-all(bf16[64,6,4096]{2,1,0:T(8,128)(2,1)} %reshape.99), channel_id=1, replica_groups=mesh['sect'=2,'dev'=64,'cores'=2] {'dev'}, dimensions={0} | all-to-all | bytes 6291456 | tf_op jit(solution)/shard_map/all_to_all | solution.py:82
  127.1 5.7 %reshape.100 = bf16[384,4096]{1,0:T(8,128)(2,1)} reshape(bf16[64,6,4096]{2,1,0:T(8,128)(2,1)} %all_to_all.10) | data formatting | bytes 6291456 | tf_op jit(solution)/shard_map/reshape | solution.py:85
  132.9 83.5 %all-gather.2.cloned.1.call-done = bf16[768,4096]{1,0:T(8,128)(2,1)} async-done(((bf16[384,4096]{1,0:T(8,128)(2,1)}), bf16[768,4096]{1,0:T(8,128)(2,1)}) %all-gather.2.cloned.1.call-update) | async-done | bytes 6291472 | tf_op jit(solution)/shard_map/all_gather | solution.py:91
  216.4 6.6 %fusion.2 = f32[768,384]{1,0:T(8,128)S(1)} fusion(bf16[768,4096]{1,0:T(8,128)(2,1)} %all-gather.2.cloned.1.call-done, bf16[1,4096,384]{2,1,0:T(8,128)(2,1)} %param.21), kind=kOutput, calls=%fused_computation.4 | convolution fusion | flops 2415919104 | bytes 10616832 | tf_op jit(solution)/shard_map/dot_general | solution.py:92
  223.0 3.5 fusion.14
  226.6 6.4 %fusion.39 = f32[2,384,2,2048]{3,1,2,0:T(8,128)} fusion(bf16[2,384,384,1]{2,1,3,0:T(8,128)(2,1)S(1)} %bitcast.83, bf16[2,2048,384,1]{2,1,0,3:T(8,128)(2,1)S(1)} %bitcast.79), kind=kOutput, calls=%fused_computation.49 | convolution fusion | flops 2415919104 | bytes 16318464 | tf_op jit(solution)/shard_map/snf,cdf->scnd/dot_general | solution.py:95
  233.0 110.7 %reduce-scatter.2.cloned.1.call-done = f32[384,2048]{1,0:T(8,128)} async-done(((f32[1536,2048]{1,0:T(8,128)}), f32[384,2048]{1,0:T(8,128)}) %reduce-scatter.2.cloned.1.call-update) | async-done | bytes 3145744 | tf_op jit(solution)/shard_map/reduce_scatter | solution.py:101
  343.8 3.3 convert_element_type.40
  347.0 3.7 reshape.103
  350.7 11.8 %all-to-all-start.1 = ((bf16[64,6,2048]{2,1,0:T(8,128)(2,1)}), bf16[64,6,2048]{2,1,0:T(8,128)(2,1)}, u32[]{:S(2)}, u32[]{:S(2)}) async-start(bf16[64,6,2048]{2,1,0:T(8,128)(2,1)} %reshape.103), calls=%async_computation.2 | async-start | bytes 4194304 | tf_op jit(solution)/shard_map/all_to_all | solution.py:108
  362.6 0.7 reshape.123
  363.3 0.7 reshape.105
  364.1 0.2 fusion.38
  364.3 2.6 fusion.37
  367.0 0.4 fusion.29
  367.4 0.6 fusion.26
  368.0 0.8 copy.62
  368.8 0.1 reshape.109
  368.9 0.1 copy.31
  369.0 43.7 %all-to-all-done.1 = bf16[64,6,2048]{2,1,0:T(8,128)(2,1)} async-done(((bf16[64,6,2048]{2,1,0:T(8,128)(2,1)}), bf16[64,6,2048]{2,1,0:T(8,128)(2,1)}, u32[]{:S(2)}, u32[]{:S(2)}) %all-to-all-start.1) | async-done | bytes 1572896 | tf_op jit(solution)/shard_map/all_to_all | solution.py:108
  412.6 3.7 reshape.104
  416.3 4.4 %gather_fusion = bf16[192,2048]{1,0:T(8,128)(2,1)} fusion(bf16[384,2048]{1,0:T(8,128)(2,1)} %reshape.104, s32[1024]{0:T(1024)S(1)} %pad_clamp_fusion), kind=kCustom, calls=%fused_computation | custom fusion | bytes 1573632 | tf_op jit(solution)/shard_map/gather | solution.py:110
  420.7 2.5 fusion.10
  (29 shorter events, 0.4 us)
Async XLA Ops:
  7.2 219.4 %copy-start = (bf16[1,4096,384]{2,1,0:T(8,128)(2,1)S(1)}, bf16[1,4096,384]{2,1,0:T(8,128)(2,1)}, u32[]{:S(2)}) copy-start(bf16[1,4096,384]{2,1,0:T(8,128)(2,1)} %param.23) | copy-start | bytes 9437188
  7.2 209.3 %all-gather.2.cloned.1.call-start = ((), (), s32[]{:S(2)}) async-start(), calls=%async_computation.3 | async-start | bytes 9437184 | tf_op jit(solution)/shard_map/all_gather | solution.py:91
  132.8 210.9 %reduce-scatter.2.cloned.1.call-start = ((), (), s32[]{:S(2)}) async-start(), calls=%async_computation.4 | async-start | bytes 15728640 | tf_op jit(solution)/shard_map/reduce_scatter | solution.py:101
  216.4 6.6 %copy-start.4 = (bf16[768,4096]{1,0:T(8,128)(2,1)S(1)}, bf16[768,4096]{1,0:T(8,128)(2,1)}, u32[]{:S(2)}) copy-start(bf16[768,4096]{1,0:T(8,128)(2,1)} %all-gather.2.cloned.1.call-done) | copy-start | bytes 18874372
  216.4 6.6 %copy-start.5 = (bf16[1,4096,384]{2,1,0:T(8,128)(2,1)S(1)}, bf16[1,4096,384]{2,1,0:T(8,128)(2,1)}, u32[]{:S(2)}) copy-start(bf16[1,4096,384]{2,1,0:T(8,128)(2,1)} %param.22) | copy-start | bytes 9437188
  350.7 11.8 %copy-start.1 = (bf16[24,4096]{1,0:T(8,128)(2,1)S(1)}, bf16[24,4096]{1,0:T(8,128)(2,1)}, u32[]{:S(2)}) copy-start(bf16[24,4096]{1,0:T(8,128)(2,1)} %param.12) | copy-start | bytes 589828
  350.7 13.3 %copy-start.3 = (s32[24]{0:T(128)S(1)}, s32[24]{0:T(128)}, u32[]{:S(2)}) copy-start(s32[24]{0:T(128)} %param.17) | copy-start | bytes 292
  350.7 61.9 %all-to-all-start.1 = ((bf16[64,6,2048]{2,1,0:T(8,128)(2,1)}), bf16[64,6,2048]{2,1,0:T(8,128)(2,1)}, u32[]{:S(2)}, u32[]{:S(2)}) async-start(bf16[64,6,2048]{2,1,0:T(8,128)(2,1)} %reshape.103), calls=%async_computation.2 | async-start | bytes 4194304 | tf_op jit(solution)/shard_map/all_to_all | solution.py:108
  364.0 3.3 copy-start.6
  367.4 1.5 copy-start.2
Sparse Core Ops, SparseCore 0:
  133.0 83.4 all-gather.1
  233.1 110.5 reduce-scatter.1
where the time goes:
time: 431 us; the launch traced here: 430 us
  waiting for transfers between devices  238 us (55%)
  blocking collectives  108 us (25%)
  local copies, waits for them, and re-layouts  26.8 us (6%)
  matrix products  23.6 us (5%)
  between operations  14.2 us (3%)
  starting transfers between devices  11.9 us (3%)
  other arithmetic  7.25 us (2%)
    reduce_scatter x1, waiting for transfers between devices, per_device(): lax.psum_scatter(terms.reshape(sections * cores * slots_all, half), ('sec...  111 us
    all_to_all x1, blocking collectives, per_device(): lax.all_to_all(outgoing.reshape(experts, capacity, width), 'dev', split_a...  108 us
    all_gather x1, waiting for transfers between devices, per_device(): piece = lax.all_gather(local_rows, 'sect', axis=0, tiled=True)  83.5 us
    all_to_all x1, waiting for transfers between devices, per_device(): lax.all_to_all(result, 'dev', split_axis=0, concat_axis=0, tiled=True)  43.7 us
    all_to_all x1, starting transfers between devices, per_device(): lax.all_to_all(result, 'dev', split_axis=0, concat_axis=0, tiled=True)  11.8 us
  transfers between devices with their start and end apart: 3, of which 3 were waited for; matrix products, arithmetic and copies ran while one was open for 1% of the time, Pallas kernels for 0%

commit v1 on v0

v1 whole, which is shorter than its diff:
```python
import functools

import jax
import jax.numpy as jnp
from jax import lax
from jax.experimental import pallas as pl
from jax.experimental.pallas import tpu as pltpu
from jax.sharding import PartitionSpec as P

MESH = pl.DeviceIdType.MESH
HD = 128
NX, NY, NZ = 4, 4, 8
R = 24
RP = 32
CAP = 6
S = NZ * CAP
W = 256
F32 = jnp.float32
BF16 = jnp.bfloat16


def dot(a, b):
    return jnp.dot(a, b, preferred_element_type=F32)


def dot_nt(a, b):
    return lax.dot_general(a, b, (((1,), (1,)), ((), ())), preferred_element_type=F32)


def wait_bytes(ref, sem):
    pltpu.make_async_copy(ref, ref, sem).wait()


def body(
    nc,
    hid, routes, gates, lens, query, new_k, new_v, keys_h, vals_h, wg_h, wu_h, wd_h,
    att_out, out,
    zb, cb, ct, pick, wtab, whl, ps, ob, xf, xo, gacc, uacc, act,
    so, ro, sx, rx, sy, ry, sz, rz, wg, wu, wd, keys, vals, qs, os, nk, nv,
    send, recv, loc,
):
    half = nc * W
    sect = lax.axis_index("sect")
    dev = lax.axis_index("dev")
    core = lax.axis_index("cores")
    xlo = lax.rem(dev // NZ, 2)
    x = sect * 2 + xlo
    y = dev // (2 * NZ)
    z = lax.rem(dev, NZ)

    def at(dx=0, dy=0, dz=0, dc=0):
        px = lax.rem(x + dx, NX)
        py = lax.rem(y + dy, NY)
        pz = lax.rem(z + dz, NZ)
        pc = lax.rem(core + dc, 2)
        return (px // 2, (py * 2 + lax.rem(px, 2)) * NZ + pz, pc)

    def push(src, dst, stage, c, to):
        pltpu.make_async_remote_copy(
            src_ref=src, dst_ref=dst, send_sem=send.at[stage, c], recv_sem=recv.at[stage, c],
            device_id=to, device_id_type=MESH,
        ).start()

    loads = [
        pltpu.make_async_copy(a, b, loc.at[i])
        for i, (a, b) in enumerate(
            ((keys_h, keys), (vals_h, vals), (wg_h, wg), (wu_h, wu), (wd_h, wd))
        )
    ]
    for load in loads:
        load.start()

    peers = (
        [at(dz=k) for k in range(1, NZ)]
        + [at(dy=k) for k in range(1, NY)]
        + [at(dx=k) for k in range(1, NX)]
        + [at(dc=1)]
    )
    barrier = pltpu.get_barrier_semaphore()
    for peer in peers:
        pl.semaphore_signal(barrier, inc=1, device_id=peer, device_id_type=MESH)

    lane = lax.broadcasted_iota(jnp.int32, (R, 128), 1)
    named = jnp.zeros((R, 128), F32)
    weight = jnp.zeros((R, 128), F32)
    for k in range(routes.shape[1]):
        route = routes[:, k : k + 1]
        named = named + jnp.where(lane == route, 1.0, 0.0)
        weight = weight + jnp.where(lane == route + 64, gates[:, k : k + 1], 0.0)
    row_i = lax.broadcasted_iota(jnp.int32, (R, R), 0)
    col_i = lax.broadcasted_iota(jnp.int32, (R, R), 1)
    earlier = dot(jnp.where(col_i < row_i, 1.0, 0.0).astype(BF16), named.astype(BF16))
    code = jnp.where(lane < 64, jnp.where(named > 0.5, earlier, -1.0), weight)
    lane_p = lax.broadcasted_iota(jnp.int32, (RP - R, 128), 1)
    cb[0] = jnp.concatenate([code, jnp.where(lane_p < 64, -1.0, 0.0)], axis=0)

    def stage_rows(c, _):
        cols = pl.ds(pl.multiple_of(core * half + c * W, W), W)
        rows = hid[:, cols].astype(F32)
        zb[c, 0] = jnp.concatenate([rows, jnp.zeros((RP - R, W), F32)], axis=0).astype(BF16)
        return 0

    lax.fori_loop(0, nc, stage_rows, 0)

    pl.semaphore_wait(barrier, len(peers))

    z_order = (4, 1, 7, 2, 6, 3, 5)
    for k in z_order:
        push(cb.at[0], cb.at[NZ - k], 8, 0, at(dz=k))

    def send_z(c, _):
        for k in z_order:
            push(zb.at[c, 0], zb.at[c, NZ - k], 0, c, at(dz=k))
        return 0

    lax.fori_loop(0, nc, send_z, 0)

    nk[...] = new_k[...].astype(F32)
    nv[...] = new_v[...].astype(F32)
    heads = query.shape[1] // HD
    for h in range(heads):
        qs[:, h, :] = query[:, h * HD : (h + 1) * HD].astype(F32)

    wait_bytes(cb.at[pl.ds(1, NZ - 1)], recv.at[8, 0])
    ct[...] = cb[...].reshape(NZ * RP, 128).T
    slot_i = lax.broadcasted_iota(jnp.int32, (S, NZ * RP), 0)
    slot_b = slot_i // CAP
    slot_s = (slot_i - slot_b * CAP).astype(F32)
    here = slot_b == lax.broadcasted_iota(jnp.int32, (S, NZ * RP), 1) // RP
    for d in range(NY):
        for q in range(2):
            expert = (lax.rem(y + d, NY) * 2 + lax.rem(xlo + q, 2)) * NZ + z
            mask = here & (ct[pl.ds(expert, 1), :] == slot_s)
            at_row = (d * 2 + q) * S
            pick[at_row : at_row + S, :] = jnp.where(mask, 1.0, 0.0).astype(BF16)
            wtab[at_row : at_row + S, :] = jnp.where(mask, ct[pl.ds(expert + 64, 1), :], 0.0)
    weights = wtab[...].T
    high = weights.astype(BF16)
    whl[0] = high
    whl[1] = (weights - high.astype(F32)).astype(BF16)

    gacc[...] = jnp.zeros_like(gacc)
    uacc[...] = jnp.zeros_like(uacc)

    scale = HD ** (-0.5)

    def attend(r):
        length = lens[r]
        q = qs[r]
        q0, q1 = q[: heads // 2], q[heads // 2 :]
        empty = jnp.zeros_like(q0)
        wide = jnp.concatenate(
            [jnp.concatenate([q0, empty], axis=1), jnp.concatenate([empty, q1], axis=1)], axis=0
        ).astype(BF16)
        scores = dot_nt(wide, keys[r]) * scale
        valid = lax.broadcasted_iota(jnp.int32, scores.shape, 1) < length
        scores = jnp.where(valid, scores, -jnp.inf)
        fresh_k = nk[pl.ds(r, 1), :]
        fresh_v = nv[pl.ds(r, 1), :]
        own = jnp.concatenate(
            [
                jnp.sum(q0 * fresh_k[:, :HD], axis=1, keepdims=True),
                jnp.sum(q1 * fresh_k[:, HD:], axis=1, keepdims=True),
            ],
            axis=0,
        ) * scale
        top = jnp.maximum(jnp.max(scores, axis=1, keepdims=True), own)
        probs = jnp.exp(scores - top)
        own_p = jnp.exp(own - top)
        total = jnp.sum(probs, axis=1, keepdims=True) + own_p
        probs_b = (probs / total).astype(BF16)
        own_b = (own_p / total).astype(BF16).astype(F32)
        mixed = dot(probs_b, vals[r])
        n = heads // 2
        os[r, :n] = mixed[:n, :HD] + own_b[:n] * fresh_v[:, :HD]
        os[r, n:] = mixed[n:, HD:] + own_b[n:] * fresh_v[:, HD:]

    per_step = R // nc
    half_rows = NX * NY * S // 2

    def gate_up(x_ref, c, base):
        depth = pl.ds(pl.multiple_of(base + c * W, W), W)

        def part(i, _):
            rows = pl.ds(pl.multiple_of(i * half_rows, half_rows), half_rows)
            block = x_ref[c, pl.ds(i * 2, 2)].reshape(half_rows, W)
            gacc[rows, :] += dot(block, wg[depth, :])
            uacc[rows, :] += dot(block, wu[depth, :])
            return 0

        lax.fori_loop(0, 2, part, 0)

    def forward(t, _):
        @pl.when(t < nc)
        def _():
            c = t
            wait_bytes(zb.at[c, pl.ds(1, NZ - 1)], recv.at[0, c])
            chosen = dot(pick[...], zb[c].reshape(NZ * RP, W)).astype(BF16)
            chosen = chosen.reshape(NY, 2, S, W)
            for d in range(1, NY):
                ps[c, d - 1] = chosen[d]
                push(ps.at[c, d - 1, 0], xf.at[c, 0, NY - d], 1, c, at(dy=d))
                push(ps.at[c, d - 1, 1], ob.at[c, NY - d], 2, c, at(dy=d))
            xf[c, 0, 0] = chosen[0, 0]
            ob[c, 0] = chosen[0, 1]

        @pl.when((t >= 1) & (t < nc + 1))
        def _():
            c = t - 1
            wait_bytes(xf.at[c, 0, pl.ds(1, NY - 1)], recv.at[1, c])
            wait_bytes(ob.at[c, pl.ds(1, NY - 1)], recv.at[2, c])
            push(xf.at[c, 0], xf.at[c, 2], 3, c, at(dx=2))
            push(ob.at[c], xf.at[c, 3], 3, c, at(dx=1))
            push(ob.at[c], xf.at[c, 1], 3, c, at(dx=3))

        @pl.when((t >= 2) & (t < nc + 2))
        def _():
            c = t - 2
            wait_bytes(xf.at[c, pl.ds(1, NX - 1)], recv.at[3, c])
            push(xf.at[c], xo.at[c], 4, c, at(dc=1))
            gate_up(xf, c, core * half)

        @pl.when(t >= 3)
        def _():
            c = t - 3
            wait_bytes(xo.at[c], recv.at[4, c])
            gate_up(xo, c, (1 - core) * half)

        @pl.when(t < nc)
        def _():
            for i in range(per_step):
                attend(t * per_step + i)

        return 0

    for load in loads[:4]:
        load.wait()
    lax.fori_loop(0, nc + 3, forward, 0)

    def activate(i, _):
        rows = pl.ds(pl.multiple_of(i * S, S), S)
        gate = gacc[rows, :]
        act[rows, :] = (gate * jax.nn.sigmoid(gate) * uacc[rows, :]).astype(BF16)
        return 0

    lax.fori_loop(0, NX * NY, activate, 0)
    loads[4].wait()

    def down(c, base, i):
        depth = pl.ds(pl.multiple_of(base + c * W, W), W)
        rows = pl.ds(pl.multiple_of(i * half_rows, half_rows), half_rows)
        return dot_nt(act[rows, :], wd[depth, :])

    def backward(t, _):
        @pl.when(t < nc)
        def _():
            c = t

            def part(i, _):
                got = down(c, (1 - core) * half, i)
                so[c, pl.ds(i * 2, 2)] = got.astype(BF16).reshape(2, NY, S, W)
                return 0

            lax.fori_loop(0, 2, part, 0)
            push(so.at[c], ro.at[c], 5, c, at(dc=1))

        @pl.when((t >= 1) & (t < nc + 1))
        def _():
            c = t - 1
            wait_bytes(ro.at[c], recv.at[5, c])

            def part(i, _):
                got = down(c, core * half, i) + ro[c, pl.ds(i * 2, 2)].reshape(
                    half_rows, W
                ).astype(F32)
                sx[c, pl.ds(i * 2, 2)] = got.astype(BF16).reshape(2, NY, S, W)
                return 0

            lax.fori_loop(0, 2, part, 0)
            push(sx.at[c, 2], rx.at[c, 2], 6, c, at(dx=2))
            push(sx.at[c, 1], rx.at[c, 0], 6, c, at(dx=1))
            push(sx.at[c, 3], rx.at[c, 1], 6, c, at(dx=3))

        @pl.when((t >= 2) & (t < nc + 2))
        def _():
            c = t - 2
            wait_bytes(rx.at[c], recv.at[6, c])
            for j in range(NY):
                mine = (sx[c, 0, j].astype(F32) + rx[c, 2, j].astype(F32)).astype(BF16)
                other = (rx[c, 0, j].astype(F32) + rx[c, 1, j].astype(F32)).astype(BF16)
                if j == 0:
                    ry[c, 0, 0] = mine
                    ry[c, 0, 1] = other
                else:
                    sy[c, j - 1, 0] = mine
                    sy[c, j - 1, 1] = other
                    push(sy.at[c, j - 1], ry.at[c, NY - j], 7, c, at(dy=j))

        @pl.when((t >= 3) & (t < nc + 3))
        def _():
            c = t - 3
            wait_bytes(ry.at[c, pl.ds(1, NY - 1)], recv.at[7, c])
            slots = ry[c].reshape(NY * 2 * S, W)
            sums = dot(whl[0], slots) + dot(whl[1], slots)
            sz[c] = sums.astype(BF16).reshape(NZ, RP, W)
            for k in z_order:
                push(sz.at[c, k], rz.at[c, NZ - k - 1], 9, c, at(dz=k))

        @pl.when(t >= 4)
        def _():
            c = t - 4
            wait_bytes(rz.at[c], recv.at[9, c])
            total = sz[c, 0].astype(F32)
            for k in range(NZ - 1):
                total = total + rz[c, k].astype(F32)
            cols = pl.ds(pl.multiple_of(c * W, W), W)
            out[:, cols] = total[:R].astype(BF16)

        return 0

    lax.fori_loop(0, nc + 4, backward, 0)

    for h in range(heads):
        att_out[:, h * HD : (h + 1) * HD] = os[:, h, :].astype(BF16)

    def drain(c, _):
        wait_bytes(zb.at[c, pl.ds(1, NZ - 1)], send.at[0, c])
        wait_bytes(xf.at[c, 0, pl.ds(1, NY - 1)], send.at[1, c])
        wait_bytes(ob.at[c, pl.ds(1, NY - 1)], send.at[2, c])
        wait_bytes(xf.at[c, pl.ds(1, NX - 1)], send.at[3, c])
        wait_bytes(xo.at[c], send.at[4, c])
        wait_bytes(ro.at[c], send.at[5, c])
        wait_bytes(rx.at[c], send.at[6, c])
        wait_bytes(ry.at[c, pl.ds(1, NY - 1)], send.at[7, c])
        wait_bytes(rz.at[c], send.at[9, c])
        return 0

    wait_bytes(cb.at[pl.ds(1, NZ - 1)], send.at[8, 0])
    lax.fori_loop(0, nc, drain, 0)


def per_device(
    query, cache_keys, cache_values, new_key, new_value, lengths,
    hidden, routes, gate_weights, w_gate, w_up, w_down,
):
    width = hidden.shape[1]
    nc = width // 2 // W
    inner = w_gate.shape[2]
    rows = NX * NY * S
    heads = query.shape[1] // HD
    vmem = pl.BlockSpec(memory_space=pltpu.VMEM)
    smem = pl.BlockSpec(memory_space=pltpu.SMEM)
    hbm = pl.BlockSpec(memory_space=pl.ANY)
    shapes = [
        ((nc, NZ, RP, W), BF16),
        ((NZ, RP, 128), F32),
        ((128, NZ * RP), F32),
        ((NY * 2 * S, NZ * RP), BF16),
        ((NY * 2 * S, NZ * RP), F32),
        ((2, NZ * RP, NY * 2 * S), BF16),
        ((nc, NY - 1, 2, S, W), BF16),
        ((nc, NY, S, W), BF16),
        ((nc, NX, NY, S, W), BF16),
        ((nc, NX, NY, S, W), BF16),
        ((rows, inner), F32),
        ((rows, inner), F32),
        ((rows, inner), BF16),
        ((nc, NX, NY, S, W), BF16),
        ((nc, NX, NY, S, W), BF16),
        ((nc, NX, NY, S, W), BF16),
        ((nc, NX - 1, NY, S, W), BF16),
        ((nc, NY - 1, 2, S, W), BF16),
        ((nc, NY, 2, S, W), BF16),
        ((nc, NZ, RP, W), BF16),
        ((nc, NZ - 1, RP, W), BF16),
        ((width, inner), BF16),
        ((width, inner), BF16),
        ((width, inner), BF16),
        (cache_keys.shape, BF16),
        (cache_values.shape, BF16),
        ((R, heads, HD), F32),
        ((R, heads, HD), F32),
        (new_key.shape, F32),
        (new_value.shape, F32),
    ]
    return pl.pallas_call(
        functools.partial(body, nc),
        out_shape=(
            jax.ShapeDtypeStruct(query.shape, BF16),
            jax.ShapeDtypeStruct((R, width // 2), BF16),
        ),
        in_specs=[vmem, vmem, vmem, smem, vmem, vmem, vmem, hbm, hbm, hbm, hbm, hbm],
        out_specs=(vmem, vmem),
        scratch_shapes=[pltpu.VMEM(s, t) for s, t in shapes]
        + [
            pltpu.SemaphoreType.DMA((10, nc)),
            pltpu.SemaphoreType.DMA((10, nc)),
            pltpu.SemaphoreType.DMA((5,)),
        ],
        compiler_params=pltpu.CompilerParams(
            collective_id=0, has_side_effects=True, vmem_limit_bytes=60 * 1024 * 1024
        ),
        name="experts",
    )(
        hidden, routes, gate_weights, lengths, query, new_key, new_value,
        cache_keys, cache_values, w_gate[0], w_up[0], w_down[0],
    )


def solution(mesh):
    rows = ("sect", "dev")
    cols = ("sect", "cores")
    in_specs = (
        P(rows, "cores"),
        P(rows, None, "cores"),
        P(rows, None, "cores"),
        P(rows, "cores"),
        P(rows, "cores"),
        P(rows),
        P(rows, None),
        P(rows, None),
        P(rows, None),
        P("dev", None, cols),
        P("dev", None, cols),
        P("dev", None, cols),
    )
    out_specs = (P(rows, "cores"), P(rows, "cores"))
    return jax.shard_map(
        per_device, mesh=mesh, in_specs=in_specs, out_specs=out_specs, check_vma=False
    )
```

time: 431 us -> 126 us (0.29)
  waiting for transfers between devices: 238 us -> 0 us
  Pallas kernels: 0 us -> 119 us
  blocking collectives: 108 us -> 0 us
  matrix products: 23.6 us -> 0 us
  local copies, waits for them, and re-layouts: 26.8 us -> 5.87 us
  between operations: 14.2 us -> 0.64 us
  starting transfers between devices: 11.9 us -> 0 us
  other arithmetic: 7.25 us -> 0 us
    pallas_call x0 -> x1, Pallas kernels: none -> 119 us  [per_device(): pl.pallas_call(functools.partial(body, nc), out_shape=(jax.ShapeDtypeStru...]
    reduce_scatter x1 -> x0, waiting for transfers between devices: 111 us -> none  [per_device(): lax.psum_scatter(terms.reshape(sections * cores * slots_all, half), ('sec...]
    all_to_all x1 -> x0, blocking collectives: 108 us -> none  [per_device(): lax.all_to_all(outgoing.reshape(experts, capacity, width), 'dev', split_a...]
    all_gather x1 -> x0, waiting for transfers between devices: 83.5 us -> none  [per_device(): piece = lax.all_gather(local_rows, 'sect', axis=0, tiled=True)]
    all_to_all x1 -> x0, waiting for transfers between devices: 43.7 us -> none  [per_device(): lax.all_to_all(result, 'dev', split_axis=0, concat_axis=0, tiled=True)]
    dot_general x7 -> x0, matrix products: 23.6 us -> none  [the longest x1 6.57 us: per_device(): gate = jnp.dot(piece, gate_w, preferred_element_type=jnp.float32)]
    reshape x5 -> x0, local copies, waits for them, and re-layouts: 19.4 us -> none  [the longest x1 5.69 us: per_device(): local_rows = arrived.reshape(slots_all, width)]
    all_to_all x1 -> x0, starting transfers between devices: 11.8 us -> none  [per_device(): lax.all_to_all(result, 'dev', split_axis=0, concat_axis=0, tiled=True)]
  transfers between devices with their start and end apart: 3 -> 0, of which waited for: 3 -> 0; matrix products, arithmetic and copies ran while one was open for 1% -> 0% of each run, Pallas kernels for 0% -> 0%
where the time goes in v1:
time: 126 us
  Pallas kernels  119 us (94%)
  local copies, waits for them, and re-layouts  5.87 us (5%)
    pallas_call x1, Pallas kernels, per_device(): pl.pallas_call(functools.partial(body, nc), out_shape=(jax.ShapeDtypeStru...  119 us
    unnamed x4, local copies, waits for them, and re-layouts  5.87 us

profile of v1, /device:TPU:2, one launch (start us, length us, event | category | flops | bytes accessed | tf_op | source)
XLA Modules:
  0.0 125.5 jit_solution(4727649486346098324)
XLA Ops:
  0.6 1.4 %copy.14.routes = s32[24,8]{1,0:T(8,128)} copy(s32[24,8]{0,1:T(8,128)} %param.19) | data formatting | bytes 1536 | tf_op args[7]
  2.0 1.4 %copy.15.gates = f32[24,8]{1,0:T(8,128)} copy(f32[24,8]{0,1:T(8,128)} %param.20) | data formatting | bytes 1536 | tf_op args[8]
  3.3 119.0 %experts.1 = (bf16[24,4096]{1,0:T(8,128)(2,1)}, bf16[24,2048]{1,0:T(8,128)(2,1)}) custom-call(bf16[24,4096]{1,0:T(8,128)(2,1)} %hid.1, s32[24,8]{1,0:T(8,128)} %copy.14.routes, f32[24,8]{1,0:T(8,128)} %copy.15.gates, s32[24]{0:T(128)} %lens.1, bf16[24,4096]{1,0:T(8,128)(2,1)} %query.1, bf16[24,256]{1,0:T(8,128)(2,1)} %new_k.1, bf16[24,256]{1,0:T(8,128)(2,1)} %new_v.1, ...), custom_call_target="tpu_custom_call" | custom-call | tf_op jit(solution)/shard_map/experts/pallas_call | solution.py:386
  122.4 1.6 %copy.18 = bf16[24,4096]{1,0:T(8,128)(2,1)} copy(bf16[24,4096]{1,0:T(8,128)(2,1)} %get-tuple-element.4) | data formatting | bytes 393216
  124.0 1.5 %copy.19 = bf16[24,2048]{1,0:T(8,128)(2,1)} copy(bf16[24,2048]{1,0:T(8,128)(2,1)} %get-tuple-element.5) | data formatting | bytes 196608

commit v2 on v1

v2 whole, which is shorter than its diff:
```python
import functools

import jax
import jax.numpy as jnp
from jax import lax
from jax.experimental import pallas as pl
from jax.experimental.pallas import tpu as pltpu
from jax.sharding import PartitionSpec as P

MESH = pl.DeviceIdType.MESH
HD = 128
NX, NY, NZ = 4, 4, 8
R = 24
RP = 32
CAP = 6
ZR = NZ * 2 * R
S = NZ * CAP
W = 256
F_LAGS = (2, 4, 7, 9, 10)
B_LAGS = (1, 3, 5, 7, 9, 11)
F32 = jnp.float32
BF16 = jnp.bfloat16


def dot(a, b):
    return jnp.dot(a, b, preferred_element_type=F32)


def dot_nt(a, b):
    return lax.dot_general(a, b, (((1,), (1,)), ((), ())), preferred_element_type=F32)


def wait_bytes(ref, sem):
    pltpu.make_async_copy(ref, ref, sem).wait()


def body(
    nc,
    hid, routes_t, gates_t, lens, query, new_k, new_v, keys_h, vals_h, wg_h, wu_h, wd_h,
    att_out, out,
    hs, hp, zb, cb, ct, pick, wtab, whl, ps, ob, xf, xo, gacc, uacc, act,
    so, ro, sx, rx, sy, ry, sz, r1, s2, r2, fo, fs, fr, wg, wu, wd, keys, vals, qs, os, nk, nv,
    send, recv, loc,
):
    half = nc * W
    sect = lax.axis_index("sect")
    dev = lax.axis_index("dev")
    core = lax.axis_index("cores")
    xlo = lax.rem(dev // NZ, 2)
    x = sect * 2 + xlo
    y = dev // (2 * NZ)
    z = lax.rem(dev, NZ)

    def at(dx=0, dy=0, dz=0, dc=0):
        px = lax.rem(x + dx, NX)
        py = lax.rem(y + dy, NY)
        pz = lax.rem(z + dz, NZ)
        pc = lax.rem(core + dc, 2)
        return (px // 2, (py * 2 + lax.rem(px, 2)) * NZ + pz, pc)

    def push(src, dst, stage, c, to):
        pltpu.make_async_remote_copy(
            src_ref=src, dst_ref=dst, send_sem=send.at[stage, c], recv_sem=recv.at[stage, c],
            device_id=to, device_id_type=MESH,
        ).start()

    loads = [
        pltpu.make_async_copy(a, b, loc.at[i])
        for i, (a, b) in enumerate(
            ((keys_h, keys), (vals_h, vals), (wg_h, wg), (wu_h, wu), (wd_h, wd))
        )
    ]
    for load in loads:
        load.start()

    peers = (
        [at(dz=k) for k in range(1, NZ)]
        + [at(dy=k) for k in range(1, NY)]
        + [at(dx=k) for k in range(1, NX)]
        + [at(dc=1)]
    )
    barrier = pltpu.get_barrier_semaphore()
    for peer in peers:
        pl.semaphore_signal(barrier, inc=1, device_id=peer, device_id_type=MESH)

    row_i = lax.broadcasted_iota(jnp.int32, (R, R), 0)
    col_i = lax.broadcasted_iota(jnp.int32, (R, R), 1)
    same = jnp.where(row_i == col_i, 1.0, 0.0)

    def turned(v):
        return lax.dot_general(
            same, v, (((1,), (1,)), ((), ())),
            precision=lax.Precision.HIGHEST, preferred_element_type=F32,
        )

    routes = turned(routes_t[...].astype(F32))
    gates = turned(gates_t[...])
    lane = lax.broadcasted_iota(jnp.int32, (R, 128), 1)
    lane_f = lane.astype(F32)
    named = jnp.zeros((R, 128), F32)
    weight = jnp.zeros((R, 128), F32)
    for k in range(routes.shape[1]):
        route = routes[:, k : k + 1]
        named = named + jnp.where(lane_f == route, 1.0, 0.0)
        weight = weight + jnp.where(lane_f == route + 64.0, gates[:, k : k + 1], 0.0)
    earlier = dot(jnp.where(col_i < row_i, 1.0, 0.0).astype(BF16), named.astype(BF16))
    cb[0, :R] = jnp.where(lane < 64, jnp.where(named > 0.5, earlier, -1.0), weight)

    def own_rows(c):
        cols = pl.ds(pl.multiple_of(core * half + c * W, W), W)
        return hid[:, cols].astype(F32)

    def stage_rows(c, _):
        hs[c] = jnp.concatenate([own_rows(c), jnp.zeros((RP - R, W), F32)], axis=0).astype(BF16)
        return 0

    lax.fori_loop(0, nc, stage_rows, 0)

    pl.semaphore_wait(barrier, len(peers))

    def send_rows(c, _):
        push(hs.at[c], hp.at[c], 0, c, at(dx=2))
        return 0

    push(hs.at[0], hp.at[0], 0, 0, at(dx=2))
    push(cb.at[0, pl.ds(0, R)], cb.at[0, pl.ds(R, R)], 7, 0, at(dx=2))
    lax.fori_loop(1, nc, send_rows, 0)

    nk[...] = new_k[...].astype(F32)
    nv[...] = new_v[...].astype(F32)
    heads = query.shape[1] // HD
    for h in range(heads):
        qs[:, h, :] = query[:, h * HD : (h + 1) * HD].astype(F32)
    gacc[...] = jnp.zeros_like(gacc)
    uacc[...] = jnp.zeros_like(uacc)

    wait_bytes(cb.at[0, pl.ds(R, R)], recv.at[7, 0])

    def send_codes():
        for k in (4, 1, 7, 2, 6, 3, 5):
            push(cb.at[0], cb.at[NZ - k], 7, 1, at(dz=k))

    def tables():
        wait_bytes(cb.at[pl.ds(1, NZ - 1)], recv.at[7, 1])
        ct[...] = cb[...].reshape(ZR, 128).T
        slot_i = lax.broadcasted_iota(jnp.int32, (S, ZR), 0)
        slot_b = slot_i // CAP
        slot_s = (slot_i - slot_b * CAP).astype(F32)
        place = lax.broadcasted_iota(jnp.int32, (S, ZR), 1)
        place_b = place // (2 * R)
        partner = place - place_b * (2 * R) >= R
        here = slot_b == place_b
        for d in range(NY):
            for kind in range(3):
                q = kind // 2
                expert = (lax.rem(y + d, NY) * 2 + lax.rem(xlo + q, 2)) * NZ + z
                block = partner if kind == 1 else jnp.logical_not(partner)
                mask = here & block & (ct[pl.ds(expert, 1), :] == slot_s)
                at_row = (d * 3 + kind) * S
                pick[at_row : at_row + S, :] = jnp.where(mask, 1.0, 0.0).astype(BF16)
                wtab[at_row : at_row + S, :] = jnp.where(mask, ct[pl.ds(expert + 64, 1), :], 0.0)

    scale = HD ** (-0.5)

    def attend(r):
        length = lens[r]
        q = qs[r]
        q0, q1 = q[: heads // 2], q[heads // 2 :]
        empty = jnp.zeros_like(q0)
        wide = jnp.concatenate(
            [jnp.concatenate([q0, empty], axis=1), jnp.concatenate([empty, q1], axis=1)], axis=0
        ).astype(BF16)
        scores = dot_nt(wide, keys[r]) * scale
        valid = lax.broadcasted_iota(jnp.int32, scores.shape, 1) < length
        scores = jnp.where(valid, scores, -jnp.inf)
        fresh_k = nk[pl.ds(r, 1), :]
        fresh_v = nv[pl.ds(r, 1), :]
        own = jnp.concatenate(
            [
                jnp.sum(q0 * fresh_k[:, :HD], axis=1, keepdims=True),
                jnp.sum(q1 * fresh_k[:, HD:], axis=1, keepdims=True),
            ],
            axis=0,
        ) * scale
        top = jnp.maximum(jnp.max(scores, axis=1, keepdims=True), own)
        probs = jnp.exp(scores - top)
        own_p = jnp.exp(own - top)
        total = jnp.sum(probs, axis=1, keepdims=True) + own_p
        probs_b = (probs / total).astype(BF16)
        own_b = (own_p / total).astype(BF16).astype(F32)
        mixed = dot(probs_b, vals[r])
        n = heads // 2
        os[r, :n] = mixed[:n, :HD] + own_b[:n] * fresh_v[:, :HD]
        os[r, n:] = mixed[n:, HD:] + own_b[n:] * fresh_v[:, HD:]

    per_step = R // nc
    half_rows = NX * NY * S // 2

    def gate_up(x_ref, c, base):
        depth = pl.ds(pl.multiple_of(base + c * W, W), W)

        def part(i, _):
            rows = pl.ds(pl.multiple_of(i * half_rows, half_rows), half_rows)
            block = x_ref[c, pl.ds(i * 2, 2)].reshape(half_rows, W)
            gacc[rows, :] += dot(block, wg[depth, :])
            uacc[rows, :] += dot(block, wu[depth, :])
            return 0

        lax.fori_loop(0, 2, part, 0)

    def forward(t, _):
        @pl.when(t < nc)
        def _():
            c = t
            wait_bytes(hp.at[c], recv.at[0, c])
            zb[c, 0] = jnp.concatenate([own_rows(c), hp[c].astype(F32)[:R]], axis=0).astype(BF16)
            push(zb.at[c, 0], zb.at[c, 4], 1, c, at(dz=4))
            push(zb.at[c, 0], zb.at[c, 7], 1, c, at(dz=1))
            push(zb.at[c, 0], zb.at[c, 1], 1, c, at(dz=7))

        @pl.when(t == 0)
        def _():
            send_codes()

        @pl.when((t >= F_LAGS[0]) & (t < nc + F_LAGS[0]))
        def _():
            c = t - F_LAGS[0]
            wait_bytes(zb.at[c, pl.ds(1, 3)], recv.at[1, c])
            push(zb.at[c, 4], zb.at[c, 3], 2, c, at(dz=1))
            push(zb.at[c, 4], zb.at[c, 5], 2, c, at(dz=7))
            push(zb.at[c, 7], zb.at[c, 6], 2, c, at(dz=1))
            push(zb.at[c, 1], zb.at[c, 2], 2, c, at(dz=7))

        @pl.when(t == F_LAGS[1])
        def _():
            tables()

        @pl.when((t >= F_LAGS[1]) & (t < nc + F_LAGS[1]))
        def _():
            c = t - F_LAGS[1]
            wait_bytes(zb.at[c, pl.ds(1, 4)], recv.at[2, c])
            chosen = dot(pick[...], zb[c].reshape(ZR, W)).astype(BF16)
            chosen = chosen.reshape(NY, 3, S, W)
            for d in (2, 1, 3):
                ps[c, d - 1] = chosen[d]
                push(ps.at[c, d - 1, pl.ds(0, 2)], xf.at[c, pl.ds(0, 2), NY - d], 3, c, at(dy=d))
                push(ps.at[c, d - 1, 2], ob.at[c, NY - d], 4, c, at(dy=d))
            xf[c, 0, 0] = chosen[0, 0]
            xf[c, 1, 0] = chosen[0, 1]
            ob[c, 0] = chosen[0, 2]

        @pl.when((t >= F_LAGS[2]) & (t < nc + F_LAGS[2]))
        def _():
            c = t - F_LAGS[2]
            wait_bytes(ob.at[c, pl.ds(1, NY - 1)], recv.at[4, c])
            push(ob.at[c], xf.at[c, 3], 5, c, at(dx=1))
            push(ob.at[c], xf.at[c, 2], 5, c, at(dx=3))

        @pl.when((t >= F_LAGS[3]) & (t < nc + F_LAGS[3]))
        def _():
            c = t - F_LAGS[3]
            wait_bytes(xf.at[c, pl.ds(0, 2), pl.ds(1, NY - 1)], recv.at[3, c])
            wait_bytes(xf.at[c, pl.ds(2, 2)], recv.at[5, c])
            push(xf.at[c], xo.at[c], 6, c, at(dc=1))
            gate_up(xf, c, core * half)

        @pl.when((t >= F_LAGS[4]) & (t < nc + F_LAGS[4]))
        def _():
            c = t - F_LAGS[4]
            wait_bytes(xo.at[c], recv.at[6, c])
            gate_up(xo, c, (1 - core) * half)

        @pl.when(t < nc)
        def _():
            for i in range(per_step):
                attend(t * per_step + i)

        @pl.when(t == nc)
        def _():
            weights = wtab[...].T
            high = weights.astype(BF16)
            whl[0] = high
            whl[1] = (weights - high.astype(F32)).astype(BF16)

        return 0

    for load in loads[:4]:
        load.wait()
    lax.fori_loop(0, nc + F_LAGS[-1], forward, 0)

    def activate(i, _):
        rows = pl.ds(pl.multiple_of(i * S, S), S)
        gate = gacc[rows, :]
        act[rows, :] = (gate * jax.nn.sigmoid(gate) * uacc[rows, :]).astype(BF16)
        return 0

    lax.fori_loop(0, NX * NY, activate, 0)
    loads[4].wait()

    def down(c, base, i):
        depth = pl.ds(pl.multiple_of(base + c * W, W), W)
        rows = pl.ds(pl.multiple_of(i * half_rows, half_rows), half_rows)
        return dot_nt(act[rows, :], wd[depth, :])

    def plus(a, *others):
        total = a.astype(F32)
        for b in others:
            total = total + b.astype(F32)
        return total

    def backward(t, _):
        @pl.when(t < nc)
        def _():
            c = t

            def part(i, _):
                got = down(c, (1 - core) * half, i)
                so[c, pl.ds(i * 2, 2)] = got.astype(BF16).reshape(2, NY, S, W)
                return 0

            lax.fori_loop(0, 2, part, 0)
            push(so.at[c], ro.at[c], 8, c, at(dc=1))

        @pl.when((t >= B_LAGS[0]) & (t < nc + B_LAGS[0]))
        def _():
            c = t - B_LAGS[0]
            wait_bytes(ro.at[c], recv.at[8, c])

            def part(i, _):
                theirs = ro[c, pl.ds(i * 2, 2)].reshape(half_rows, W)
                got = down(c, core * half, i) + theirs.astype(F32)
                sx[c, pl.ds(i * 2, 2)] = got.astype(BF16).reshape(2, NY, S, W)
                return 0

            lax.fori_loop(0, 2, part, 0)
            push(sx.at[c, 2], rx.at[c, 0], 9, c, at(dx=1))
            push(sx.at[c, 3], rx.at[c, 1], 9, c, at(dx=3))
            for j in (2, 1, 3):
                push(sx.at[c, pl.ds(0, 2), j], ry.at[c, NY - j, pl.ds(0, 2)], 10, c, at(dy=j))
            ry[c, 0, 0] = sx[c, 0, 0]
            ry[c, 0, 1] = sx[c, 1, 0]

        @pl.when((t >= B_LAGS[1]) & (t < nc + B_LAGS[1]))
        def _():
            c = t - B_LAGS[1]
            wait_bytes(rx.at[c], recv.at[9, c])
            for j in (2, 1, 3):
                sy[c, j - 1] = plus(rx[c, 0, j], rx[c, 1, j]).astype(BF16)
                push(sy.at[c, j - 1], ry.at[c, NY - j, 2], 11, c, at(dy=j))
            ry[c, 0, 2] = plus(rx[c, 0, 0], rx[c, 1, 0]).astype(BF16)

        @pl.when((t >= B_LAGS[2]) & (t < nc + B_LAGS[2]))
        def _():
            c = t - B_LAGS[2]
            wait_bytes(ry.at[c, pl.ds(1, NY - 1), pl.ds(0, 2)], recv.at[10, c])
            wait_bytes(ry.at[c, pl.ds(1, NY - 1), 2], recv.at[11, c])
            slots = ry[c].reshape(NY * 3 * S, W)
            sums = dot(whl[0], slots) + dot(whl[1], slots)
            sz[c] = sums.astype(BF16).reshape(NZ, 2 * R, W)
            push(sz.at[c, 6], r1.at[c, 0], 12, c, at(dz=7))
            push(sz.at[c, 2], r1.at[c, 1], 12, c, at(dz=1))
            push(sz.at[c, 5], r1.at[c, 2], 12, c, at(dz=1))
            push(sz.at[c, 3], r1.at[c, 3], 12, c, at(dz=7))

        @pl.when((t >= B_LAGS[3]) & (t < nc + B_LAGS[3]))
        def _():
            c = t - B_LAGS[3]
            wait_bytes(r1.at[c], recv.at[12, c])
            s2[c, 2] = plus(sz[c, 4], r1[c, 2], r1[c, 3]).astype(BF16)
            push(s2.at[c, 2], r2.at[c, 2], 13, c, at(dz=4))
            s2[c, 0] = plus(sz[c, 7], r1[c, 0]).astype(BF16)
            push(s2.at[c, 0], r2.at[c, 0], 13, c, at(dz=7))
            s2[c, 1] = plus(sz[c, 1], r1[c, 1]).astype(BF16)
            push(s2.at[c, 1], r2.at[c, 1], 13, c, at(dz=1))

        @pl.when((t >= B_LAGS[4]) & (t < nc + B_LAGS[4]))
        def _():
            c = t - B_LAGS[4]
            wait_bytes(r2.at[c], recv.at[13, c])
            total = plus(sz[c, 0], r2[c, 0], r2[c, 1], r2[c, 2])
            fo[c] = total[:R]
            fs[c] = jnp.concatenate([total[R:], jnp.zeros((RP - R, W), F32)], axis=0).astype(BF16)
            push(fs.at[c], fr.at[c], 14, c, at(dx=2))

        @pl.when((t >= B_LAGS[5]) & (t < nc + B_LAGS[5]))
        def _():
            c = t - B_LAGS[5]
            wait_bytes(fr.at[c], recv.at[14, c])
            cols = pl.ds(pl.multiple_of(c * W, W), W)
            out[:, cols] = (fo[c] + fr[c].astype(F32)[:R]).astype(BF16)

        @pl.when(t == 2)
        def _():
            for h in range(heads):
                att_out[:, h * HD : (h + 1) * HD] = os[:, h, :].astype(BF16)

        return 0

    lax.fori_loop(0, nc + B_LAGS[-1], backward, 0)

    def drain(c, _):
        wait_bytes(hp.at[c], send.at[0, c])
        wait_bytes(zb.at[c, pl.ds(1, 3)], send.at[1, c])
        wait_bytes(zb.at[c, pl.ds(1, 4)], send.at[2, c])
        wait_bytes(xf.at[c, pl.ds(0, 2), pl.ds(1, NY - 1)], send.at[3, c])
        wait_bytes(ob.at[c, pl.ds(1, NY - 1)], send.at[4, c])
        wait_bytes(xf.at[c, pl.ds(2, 2)], send.at[5, c])
        wait_bytes(xo.at[c], send.at[6, c])
        wait_bytes(ro.at[c], send.at[8, c])
        wait_bytes(rx.at[c], send.at[9, c])
        wait_bytes(ry.at[c, pl.ds(1, NY - 1), pl.ds(0, 2)], send.at[10, c])
        wait_bytes(ry.at[c, pl.ds(1, NY - 1), 2], send.at[11, c])
        wait_bytes(r1.at[c], send.at[12, c])
        wait_bytes(r2.at[c], send.at[13, c])
        wait_bytes(fr.at[c], send.at[14, c])
        return 0

    wait_bytes(cb.at[0, pl.ds(R, R)], send.at[7, 0])
    wait_bytes(cb.at[pl.ds(1, NZ - 1)], send.at[7, 1])
    lax.fori_loop(0, nc, drain, 0)


def per_device(
    query, cache_keys, cache_values, new_key, new_value, lengths,
    hidden, routes, gate_weights, w_gate, w_up, w_down,
):
    width = hidden.shape[1]
    nc = width // 2 // W
    inner = w_gate.shape[2]
    rows = NX * NY * S
    heads = query.shape[1] // HD
    vmem = pl.BlockSpec(memory_space=pltpu.VMEM)
    smem = pl.BlockSpec(memory_space=pltpu.SMEM)
    hbm = pl.BlockSpec(memory_space=pl.ANY)
    shapes = [
        ((nc, RP, W), BF16),
        ((nc, RP, W), BF16),
        ((nc, NZ, 2 * R, W), BF16),
        ((NZ, 2 * R, 128), F32),
        ((128, ZR), F32),
        ((NY * 3 * S, ZR), BF16),
        ((NY * 3 * S, ZR), F32),
        ((2, ZR, NY * 3 * S), BF16),
        ((nc, NY - 1, 3, S, W), BF16),
        ((nc, NY, S, W), BF16),
        ((nc, NX, NY, S, W), BF16),
        ((nc, NX, NY, S, W), BF16),
        ((rows, inner), F32),
        ((rows, inner), F32),
        ((rows, inner), BF16),
        ((nc, NX, NY, S, W), BF16),
        ((nc, NX, NY, S, W), BF16),
        ((nc, NX, NY, S, W), BF16),
        ((nc, 2, NY, S, W), BF16),
        ((nc, NY - 1, S, W), BF16),
        ((nc, NY, 3, S, W), BF16),
        ((nc, NZ, 2 * R, W), BF16),
        ((nc, 4, 2 * R, W), BF16),
        ((nc, 3, 2 * R, W), BF16),
        ((nc, 3, 2 * R, W), BF16),
        ((nc, R, W), F32),
        ((nc, RP, W), BF16),
        ((nc, RP, W), BF16),
        ((width, inner), BF16),
        ((width, inner), BF16),
        ((width, inner), BF16),
        (cache_keys.shape, BF16),
        (cache_values.shape, BF16),
        ((R, heads, HD), F32),
        ((R, heads, HD), F32),
        (new_key.shape, F32),
        (new_value.shape, F32),
    ]
    return pl.pallas_call(
        functools.partial(body, nc),
        out_shape=(
            jax.ShapeDtypeStruct(query.shape, BF16),
            jax.ShapeDtypeStruct((R, width // 2), BF16),
        ),
        in_specs=[vmem, vmem, vmem, smem, vmem, vmem, vmem, hbm, hbm, hbm, hbm, hbm],
        out_specs=(vmem, vmem),
        scratch_shapes=[pltpu.VMEM(s, t) for s, t in shapes]
        + [
            pltpu.SemaphoreType.DMA((15, nc)),
            pltpu.SemaphoreType.DMA((15, nc)),
            pltpu.SemaphoreType.DMA((5,)),
        ],
        compiler_params=pltpu.CompilerParams(
            collective_id=0, has_side_effects=True, vmem_limit_bytes=60 * 1024 * 1024
        ),
        name="experts",
    )(
        hidden, routes.T, gate_weights.T, lengths, query, new_key, new_value,
        cache_keys, cache_values, w_gate[0], w_up[0], w_down[0],
    )


def solution(mesh):
    rows = ("sect", "dev")
    cols = ("sect", "cores")
    in_specs = (
        P(rows, "cores"),
        P(rows, None, "cores"),
        P(rows, None, "cores"),
        P(rows, "cores"),
        P(rows, "cores"),
        P(rows),
        P(rows, None),
        P(rows, None),
        P(rows, None),
        P("dev", None, cols),
        P("dev", None, cols),
        P("dev", None, cols),
    )
    out_specs = (P(rows, "cores"), P(rows, "cores"))
    return jax.shard_map(
        per_device, mesh=mesh, in_specs=in_specs, out_specs=out_specs, check_vma=False
    )
```

time: 126 us -> 115 us (0.913)
  Pallas kernels: 119 us -> 111 us
  local copies, waits for them, and re-layouts: 5.87 us -> 3.16 us
    pallas_call x1, Pallas kernels: 119 us -> 111 us  [per_device(): pl.pallas_call(functools.partial(body, nc), out_shape=(jax.ShapeDtypeStru...]
    unnamed x4 -> x2, local copies, waits for them, and re-layouts: 5.87 us -> 3.16 us
where the time goes in v2:
time: 115 us; the launch traced here: 114 us
  Pallas kernels  111 us (97%)
  local copies, waits for them, and re-layouts  3.16 us (3%)
    pallas_call x1, Pallas kernels, per_device(): pl.pallas_call(functools.partial(body, nc), out_shape=(jax.ShapeDtypeStru...  111 us
    unnamed x2, local copies, waits for them, and re-layouts  3.16 us

profile of v2, /device:TPU:2, one launch (start us, length us, event | category | flops | bytes accessed | tf_op | source)
XLA Modules:
  0.0 114.4 jit_solution(3343962342262259059)
XLA Ops:
  0.6 110.6 %experts.1 = (bf16[24,4096]{1,0:T(8,128)(2,1)}, bf16[24,2048]{1,0:T(8,128)(2,1)}) custom-call(bf16[24,4096]{1,0:T(8,128)(2,1)} %hid.1, s32[8,24]{1,0:T(8,128)} %bitcast.8, f32[8,24]{1,0:T(8,128)} %bitcast.9, s32[24]{0:T(128)} %lens.1, bf16[24,4096]{1,0:T(8,128)(2,1)} %query.1, bf16[24,256]{1,0:T(8,128)(2,1)} %new_k.1, bf16[24,256]{1,0:T(8,128)(2,1)} %new_v.1, ...), custom_call_target="tpu_custom_call" | custom-call | tf_op jit(solution)/shard_map/experts/pallas_call | solution.py:474
  111.2 1.6 %copy.16 = bf16[24,4096]{1,0:T(8,128)(2,1)} copy(bf16[24,4096]{1,0:T(8,128)(2,1)} %get-tuple-element.4) | data formatting | bytes 393216
  112.8 1.5 %copy.17 = bf16[24,2048]{1,0:T(8,128)(2,1)} copy(bf16[24,2048]{1,0:T(8,128)(2,1)} %get-tuple-element.5) | data formatting | bytes 196608

commit v3 on v2

--- a/solution.py
+++ b/solution.py
@@ -193,7 +193,7 @@
         os[r, :n] = mixed[:n, :HD] + own_b[:n] * fresh_v[:, :HD]
         os[r, n:] = mixed[n:, HD:] + own_b[n:] * fresh_v[:, HD:]
 
-    per_step = R // nc
+    per_step = -(-R // nc)
     half_rows = NX * NY * S // 2
 
     def gate_up(x_ref, c, base):
@@ -243,8 +243,9 @@
             chosen = chosen.reshape(NY, 3, S, W)
             for d in (2, 1, 3):
                 ps[c, d - 1] = chosen[d]
+                push(ps.at[c, d - 1, 2], ob.at[c, NY - d], 4, c, at(dy=d))
+            for d in (2, 1, 3):
                 push(ps.at[c, d - 1, pl.ds(0, 2)], xf.at[c, pl.ds(0, 2), NY - d], 3, c, at(dy=d))
-                push(ps.at[c, d - 1, 2], ob.at[c, NY - d], 4, c, at(dy=d))
             xf[c, 0, 0] = chosen[0, 0]
             xf[c, 1, 0] = chosen[0, 1]
             ob[c, 0] = chosen[0, 2]
@@ -270,10 +271,20 @@
             wait_bytes(xo.at[c], recv.at[6, c])
             gate_up(xo, c, (1 - core) * half)
 
-        @pl.when(t < nc)
+        @pl.when(t == 0)
+        def _():
+            loads[0].wait()
+            loads[1].wait()
+
+        @pl.when(t * per_step < R)
         def _():
             for i in range(per_step):
                 attend(t * per_step + i)
+
+        @pl.when(t == 1)
+        def _():
+            loads[2].wait()
+            loads[3].wait()
 
         @pl.when(t == nc)
         def _():
@@ -284,8 +295,6 @@
 
         return 0
 
-    for load in loads[:4]:
-        load.wait()
     lax.fori_loop(0, nc + F_LAGS[-1], forward, 0)
 
     def activate(i, _):
@@ -473,10 +482,7 @@
     ]
     return pl.pallas_call(
         functools.partial(body, nc),
-        out_shape=(
-            jax.ShapeDtypeStruct(query.shape, BF16),
-            jax.ShapeDtypeStruct((R, width // 2), BF16),
-        ),
+        out_shape=(pltpu.VMEM(query.shape, BF16), pltpu.VMEM((R, width // 2), BF16)),
         in_specs=[vmem, vmem, vmem, smem, vmem, vmem, vmem, hbm, hbm, hbm, hbm, hbm],
         out_specs=(vmem, vmem),
         scratch_shapes=[pltpu.VMEM(s, t) for s, t in shapes]

time: 115 us -> 112 us (0.974)
  Pallas kernels: 111 us -> 109 us
  local copies, waits for them, and re-layouts: 3.16 us -> 1.32 us
    unnamed x2, local copies, waits for them, and re-layouts: 3.16 us -> 1.32 us
where the time goes in v3:
time: 112 us; the launch traced here: 111 us
  Pallas kernels  109 us (97%)
  local copies, waits for them, and re-layouts  1.32 us (1%)
    pallas_call x1, Pallas kernels, per_device(): pl.pallas_call(functools.partial(body, nc), out_shape=(pltpu.VMEM(query.s...  109 us

profile of v3, /device:TPU:2, one launch (start us, length us, event | category | flops | bytes accessed | tf_op | source)
XLA Modules:
  0.0 111.4 jit_solution(695983296782795275)
XLA Ops:
  0.6 109.5 %experts.1 = (bf16[24,4096]{1,0:T(8,128)(2,1)S(1)}, bf16[24,2048]{1,0:T(8,128)(2,1)S(1)}) custom-call(bf16[24,4096]{1,0:T(8,128)(2,1)} %hid.1, s32[8,24]{1,0:T(8,128)} %bitcast.8, f32[8,24]{1,0:T(8,128)} %bitcast.9, s32[24]{0:T(128)} %lens.1, bf16[24,4096]{1,0:T(8,128)(2,1)} %query.1, bf16[24,256]{1,0:T(8,128)(2,1)} %new_k.1, bf16[24,256]{1,0:T(8,128)(2,1)} %new_v.1, ...), custom_call_target="tpu_custom_call" | custom-call | tf_op jit(solution)/shard_map/experts/pallas_call | solution.py:483
  110.1 0.7 copy.16
  110.8 0.6 copy.17

commit v4 on v3

--- a/solution.py
+++ b/solution.py
@@ -16,8 +16,8 @@
 ZR = NZ * 2 * R
 S = NZ * CAP
 W = 256
-F_LAGS = (2, 4, 7, 9, 10)
-B_LAGS = (1, 3, 5, 7, 9, 11)
+F_LAGS = (2, 4, 6, 8, 9)
+B_LAGS = (1, 2, 4, 6, 8, 10)
 F32 = jnp.float32
 BF16 = jnp.bfloat16
 
@@ -193,7 +193,7 @@
         os[r, :n] = mixed[:n, :HD] + own_b[:n] * fresh_v[:, :HD]
         os[r, n:] = mixed[n:, HD:] + own_b[n:] * fresh_v[:, HD:]
 
-    per_step = -(-R // nc)
+    per_step = 2
     half_rows = NX * NY * S // 2
 
     def gate_up(x_ref, c, base):

time: 112 us -> 109 us (0.973)
  Pallas kernels: 109 us -> 107 us
    pallas_call x1, Pallas kernels: 109 us -> 107 us  [per_device(): pl.pallas_call(functools.partial(body, nc), out_shape=(pltpu.VMEM(query.s...]
where the time goes in v4:
time: 109 us
  Pallas kernels  107 us (98%)
  local copies, waits for them, and re-layouts  1.32 us (1%)
    pallas_call x1, Pallas kernels, per_device(): pl.pallas_call(functools.partial(body, nc), out_shape=(pltpu.VMEM(query.s...  107 us

profile of v4, /device:TPU:2, one launch (start us, length us, event | category | flops | bytes accessed | tf_op | source)
XLA Modules:
  0.0 108.8 jit_solution(10490658363039709934)
XLA Ops:
  0.6 106.8 %experts.1 = (bf16[24,4096]{1,0:T(8,128)(2,1)S(1)}, bf16[24,2048]{1,0:T(8,128)(2,1)S(1)}) custom-call(bf16[24,4096]{1,0:T(8,128)(2,1)} %hid.1, s32[8,24]{1,0:T(8,128)} %bitcast.8, f32[8,24]{1,0:T(8,128)} %bitcast.9, s32[24]{0:T(128)} %lens.1, bf16[24,4096]{1,0:T(8,128)(2,1)} %query.1, bf16[24,256]{1,0:T(8,128)(2,1)} %new_k.1, bf16[24,256]{1,0:T(8,128)(2,1)} %new_v.1, ...), custom_call_target="tpu_custom_call" | custom-call | tf_op jit(solution)/shard_map/experts/pallas_call | solution.py:483
  107.5 0.7 copy.16
  108.2 0.6 copy.17
